TPU v7x, 32 devices: a whole 2x2x4 slice. The times are simulated.
32 devices in a mesh: groups: 2 (over x), owner: 16 (over z, y, core).
Axes of the slice: x: 2, y: 2, z: 4, core: 2. Of those that a mesh axis runs over, the one named last changes fastest.
Arguments:
- tokens: bfloat16 [512, 8192], P(('groups', 'owner')), parts along dimension 0, may hold values from -6 to 6
- base_weight: bfloat16 [2, 8192, 16384], P(None, None, 'owner'), may hold values from -0.0625 to 0.0625
- adapter_down: float32 [32, 32, 8192], P(('groups', 'owner')), parts along dimension 0, may hold values from -0.0625 to 0.0625
- adapter_up: float32 [32, 2, 16, 16384], P(('groups', 'owner')), parts along dimension 0, may hold values from -1.5 to 1.5
- adapter_id: int32 [512, 1], P('groups'), parts along dimension 0, may hold values from 0 to 15; in each aligned block of 256 rows (0 to 255, 256 to 511, ...) at most 32 rows name the same one
- owner_of: int32 [32], P('groups'), parts along dimension 0, may hold values from 0 to 15, each once
Outputs:
- hidden: bfloat16 [512, 16384], P('groups', 'owner'), parts along dimension 0
There are 2 independent parts, one for each index of `groups`. A program takes and returns all parts, laid end to end along the dimension named above; an argument that names none is the same for every part. Nothing has to cross between parts.
Inputs may be any that keep to these rules, and one draw needn't show every extreme that they name: `adapter_id`: no adapter is named by more than 32 rows of a part, a bound that some block reaches. `owner_of`: A permutation: every owner index holds exactly one adapter.
All inputs are finite; a program needn't handle non-finite values.
Results may differ from a plain program's by a relative error of at most 0.0052.
Values may be sent and summed in bfloat16 or wider, within the bound.
A program may use at most 128 MiB of HBM per device.

v0:
```python
import jax
import jax.numpy as jnp
from jax import lax
from jax.sharding import PartitionSpec as P

CAP = 32


def on_device(tokens, base_weight, adapter_down, adapter_up, adapter_id, owner_of):
    owners = lax.axis_size("owner")
    own_index = lax.axis_index("owner")
    rows_dev = tokens.shape[0]
    row_count = rows_dev * owners
    ff_dev = base_weight.shape[2]
    lowrank = adapter_up.shape[2]
    table_hits = (adapter_id[:, 0][:, None] == jnp.arange(owners, dtype=jnp.int32)[None, :]).astype(
        jnp.int32
    )
    home = jnp.sum(table_hits * owner_of[None, :], axis=1)
    member = (home[:, None] == jnp.arange(owners, dtype=jnp.int32)[None, :]).astype(jnp.int32)
    before = jnp.cumsum(member, axis=0) - member
    bucket_slot = jnp.sum(before * member, axis=1)
    mine = (home == own_index).astype(jnp.int32)
    matched = (bucket_slot[None, :] == jnp.arange(CAP, dtype=jnp.int32)[:, None]).astype(
        jnp.int32
    ) * mine[None, :]
    bucket_row = jnp.sum(matched * jnp.arange(row_count, dtype=jnp.int32)[None, :], axis=1)
    filled = jnp.sum(matched, axis=1)
    gate_weight = base_weight[0]
    up_weight = base_weight[1]
    piece = lax.all_gather(tokens, "owner", axis=0, tiled=True)
    count = piece.shape[0]
    gate_part = jnp.dot(piece, gate_weight, preferred_element_type=jnp.float32)
    up_part = jnp.dot(piece, up_weight, preferred_element_type=jnp.float32)
    gate_out = gate_part
    up_out = up_part
    inside = (bucket_row >= 0) & (bucket_row < count) & (filled > 0)
    fetched = jnp.take(piece, jnp.clip(bucket_row, 0, count - 1), axis=0)
    picked = jnp.where(inside[:, None], fetched.astype(jnp.float32), 0.0)
    gate_out, up_out, picked = (gate_out, up_out, picked)
    codes = lax.dot_general(
        picked, adapter_down[0], (((1,), (1,)), ((), ())), precision=lax.Precision.HIGHEST
    )
    factor_local = adapter_up[0].reshape(2, lowrank, owners, ff_dev)
    full_terms = jnp.einsum(
        "cpk,pkof->cpof",
        codes.reshape(CAP, 2, lowrank),
        factor_local,
        precision=lax.Precision.HIGHEST,
    )
    full_terms = full_terms.astype(jnp.bfloat16)
    received = lax.all_to_all(full_terms, "owner", split_axis=2, concat_axis=2, tiled=True)
    adapter_term = received[bucket_slot, :, home, :].astype(jnp.float32)
    gate_pre = gate_out + adapter_term[:, 0, :]
    up_pre = up_out + adapter_term[:, 1, :]
    hidden = jax.nn.silu(gate_pre) * up_pre
    return hidden.astype(jnp.bfloat16)


def solution(mesh):
    return jax.shard_map(
        on_device,
        mesh=mesh,
        in_specs=(
            P(("groups", "owner"), None),
            P(None, None, "owner"),
            P(("groups", "owner"), None, None),
            P(("groups", "owner"), None, None, None),
            P("groups", None),
            P("groups"),
        ),
        out_specs=P("groups", "owner"),
        check_vma=False,
    )
```

profile of v0, /device:TPU:13, one launch (start us, length us, event | category | flops | bytes accessed | tf_op | source)
XLA Modules:
  0.0 161.7 jit_solution(896139001530302476)
XLA Ops:
  6.5 0.0 copy-start
  6.5 0.0 all-gather.2.cloned.1.call-start
  6.5 0.7 all-gather.2.cloned.1.call-update
  7.3 0.8 select_reduce_fusion.1
  8.1 0.6 reduce-window.6
  8.6 0.2 slice_reduce_fusion
  8.9 2.8 %copy.24 = f32[4,8,16,1024]{3,2,1,0:T(8,128)S(1)} copy(f32[4,8,16,1024]{3,1,2,0:T(8,128)} %bitcast.72) | data formatting | bytes 4194304
  11.7 0.1 fusion.33
  11.8 0.1 select_reduce_fusion
  11.9 48.8 %all-gather.2.cloned.1.call-done = bf16[256,8192]{1,0:T(8,128)(2,1)} async-done(((bf16[16,8192]{1,0:T(8,128)(2,1)}), bf16[256,8192]{1,0:T(8,128)(2,1)}) %all-gather.2.cloned.1.call-update) | async-done | bytes 4194320 | tf_op jit(solution)/shard_map/all_gather | solution.py:31
  60.7 4.9 %gather_fusion = bf16[32,8192]{1,0:T(8,128)(2,1)} fusion(bf16[256,8192]{1,0:T(8,128)(2,1)} %all-gather.2.cloned.1.call-done, s32[1024]{0:T(1024)S(1)} %pad_clamp_fusion), kind=kCustom, calls=%fused_computation | custom fusion | bytes 1048704 | tf_op jit(solution)/shard_map/jit(_take)/gather | solution.py:38
  65.6 0.0 copy-done
  65.6 2.1 %convolution_bitcast_fusion = f32[32,2,16,1]{0,2,3,1:T(8,128)S(1)} fusion(f32[2,16,8192]{2,1,0:T(8,128)S(1)} %bitcast.69, bf16[32,8192]{1,0:T(8,128)(2,1)} %gather_fusion, pred[32]{0:T(512)(128)(4,1)S(1)} %get-tuple-element.8, pred[32]{0:T(512)(128)(4,1)S(1)} %get-tuple-element.7), kind=kOutput, calls=%fused_computation.15 | convolution fusion | flops 101449728 | bytes 1577024 | tf_op jit(solution)/shard_map/dot_general | solution.py:41
  67.8 4.1 %convert_bitcast_fusion = bf16[32,2,16,1024]{3,0,2,1:T(8,128)(2,1)S(1)} fusion(f32[32,2,16,1]{0,2,3,1:T(8,128)S(1)} %convolution_bitcast_fusion, f32[2,16,16,1024]{3,2,1,0:T(8,128)S(1)} %bitcast.71), kind=kOutput, calls=%fused_computation.10 | convolution fusion | flops 202375168 | bytes 4198400 | tf_op jit(solution)/shard_map/cpk,pkof->cpof/dot_general | solution.py:45
  71.9 1.5 copy.19
  73.4 4.9 %all-to-all-start = ((bf16[32,2,16,1024]{3,0,1,2:T(8,128)(2,1)}), bf16[32,2,16,1024]{3,0,1,2:T(8,128)(2,1)S(1)}, u32[]{:S(2)}, u32[]{:S(2)}) async-start(bf16[32,2,16,1024]{3,0,1,2:T(8,128)(2,1)} %copy.19), calls=%async_computation | async-start | bytes 4194304 | tf_op jit(solution)/shard_map/all_to_all | solution.py:52
  78.3 47.4 %all-to-all-done = bf16[32,2,16,1024]{3,0,1,2:T(8,128)(2,1)S(1)} async-done(((bf16[32,2,16,1024]{3,0,1,2:T(8,128)(2,1)}), bf16[32,2,16,1024]{3,0,1,2:T(8,128)(2,1)S(1)}, u32[]{:S(2)}, u32[]{:S(2)}) %all-to-all-start) | async-done | bytes 2097184 | tf_op jit(solution)/shard_map/all_to_all | solution.py:52
  125.7 3.5 %copy.20 = bf16[32,2,16,1024]{3,1,2,0:T(2,128)(2,1)} copy(bf16[32,2,16,1024]{3,0,1,2:T(8,128)(2,1)S(1)} %all-to-all-done) | data formatting | bytes 4194304 | tf_op jit(solution)/shard_map/all_to_all | solution.py:52
  129.2 4.7 %gather_fusion.1 = bf16[256,2,1024]{2,1,0:T(2,128)(2,1)S(1)} fusion(bf16[32,2,16,1024]{3,1,2,0:T(2,128)(2,1)} %copy.20, s32[256]{0:T(256)S(1)} %bitcast.70), kind=kCustom, calls=%fused_computation.1 | custom fusion | bytes 2099200 | tf_op jit(solution)/shard_map/gather | solution.py:53
  133.9 0.3 copy_convert_fusion
  134.2 0.0 copy-start.1
  134.2 9.5 %fusion.10 = f32[256,1024]{1,0:T(8,128)S(1)} fusion(bf16[256,8192]{1,0:T(8,128)(2,1)} %all-gather.2.cloned.1.call-done, bf16[2,8192,1024]{2,1,0:T(8,128)(2,1)} %param.7, f32[256,2,1024]{2,0,1:T(8,128)S(1)} %copy_convert_fusion), kind=kOutput, calls=%fused_computation.11 | convolution fusion | flops 4295229440 | bytes 23068672 | tf_op jit(solution)/shard_map/dot_general | solution.py:33
  143.7 0.0 copy-done.1
  143.8 11.2 %fusion.19 = bf16[256,1024]{1,0:T(8,128)(2,1)} fusion(bf16[256,8192]{1,0:T(8,128)(2,1)S(1)} %copy-done.1, bf16[2,8192,1024]{2,1,0:T(8,128)(2,1)} %param.7, f32[256,2,1024]{2,0,1:T(8,128)S(1)} %copy_convert_fusion, f32[256,1024]{1,0:T(8,128)S(1)} %fusion.10), kind=kOutput, calls=%fused_computation.14 | convolution fusion | flops 4296802304 | bytes 23592960 | tf_op jit(solution)/shard_map/dot_general | solution.py:34
  (8 shorter events, 0.1 us)
Async XLA Ops:
  6.5 59.1 %copy-start = (f32[1,32,8192]{2,1,0:T(8,128)S(1)}, f32[1,32,8192]{2,1,0:T(8,128)}, u32[]{:S(2)}) copy-start(f32[1,32,8192]{2,1,0:T(8,128)} %param.8) | copy-start | bytes 3145732
  6.5 54.2 %all-gather.2.cloned.1.call-start = ((), (), s32[]{:S(2)}) async-start(), calls=%async_computation.1 | async-start | bytes 4456448 | tf_op jit(solution)/shard_map/all_gather | solution.py:31
  73.4 52.3 %all-to-all-start = ((bf16[32,2,16,1024]{3,0,1,2:T(8,128)(2,1)}), bf16[32,2,16,1024]{3,0,1,2:T(8,128)(2,1)S(1)}, u32[]{:S(2)}, u32[]{:S(2)}) async-start(bf16[32,2,16,1024]{3,0,1,2:T(8,128)(2,1)} %copy.19), calls=%async_computation | async-start | bytes 4194304 | tf_op jit(solution)/shard_map/all_to_all | solution.py:52
  134.2 9.5 %copy-start.1 = (bf16[256,8192]{1,0:T(8,128)(2,1)S(1)}, bf16[256,8192]{1,0:T(8,128)(2,1)}, u32[]{:S(2)}) copy-start(bf16[256,8192]{1,0:T(8,128)(2,1)} %all-gather.2.cloned.1.call-done) | copy-start | bytes 12582916
Sparse Core Ops, SparseCore 0:
  9.5 51.1 all-gather.1
where the time goes:
time: 162 us
  waiting for transfers between devices  96.9 us (60%)
  matrix products  27 us (17%)
  local copies, waits for them, and re-layouts  17.5 us (11%)
  between operations  13.5 us (8%)
  starting transfers between devices  4.88 us (3%)
  other arithmetic  1.98 us (1%)
    all_gather x1, waiting for transfers between devices, on_device(): piece = lax.all_gather(tokens, 'owner', axis=0, tiled=True)  48.8 us
    all_to_all x1, waiting for transfers between devices, on_device(): lax.all_to_all(full_terms, 'owner', split_axis=2, concat_axis=2, tiled=True)  47.4 us
    dot_general x1, matrix products, on_device(): up_part = jnp.dot(piece, up_weight, preferred_element_type=jnp.float32)  11.2 us
    dot_general x1, matrix products, on_device(): gate_part = jnp.dot(piece, gate_weight, preferred_element_type=jnp.float32)  9.52 us
    all_to_all x1, starting transfers between devices, on_device(): lax.all_to_all(full_terms, 'owner', split_axis=2, concat_axis=2, tiled=True)  4.88 us
    gather x1, local copies, waits for them, and re-layouts, on_device(): fetched = jnp.take(piece, jnp.clip(bucket_row, 0, count - 1), axis=0)  4.86 us
    gather x1, local copies, waits for them, and re-layouts, on_device(): adapter_term = received[bucket_slot, :, home, :].astype(jnp.float32)  4.65 us
    dot_general x1, matrix products, on_device(): jnp.einsum('cpk,pkof->cpof', codes.reshape(CAP, 2, lowrank), factor_local...  4.14 us
  transfers between devices with their start and end apart: 2, of which 2 were waited for; matrix products, arithmetic and copies ran while one was open for 3% of the time, Pallas kernels for 0%

commit v1 on v0

v1 whole, which is shorter than its diff:
```python
import functools

import jax
import jax.numpy as jnp
from jax import lax
from jax.experimental import pallas as pl
from jax.experimental.pallas import tpu as pltpu
from jax.sharding import PartitionSpec as P

CAP = 32
CHUNKS = 4
COLUMN_TILE = 256
HIGHEST = lax.Precision.HIGHEST


def on_device(tokens, base_weight, adapter_down, adapter_up, adapter_id, owner_of):
    owners = lax.axis_size("owner")
    own_index = lax.axis_index("owner")
    rows_dev = tokens.shape[0]
    row_count = rows_dev * owners
    ff_dev = base_weight.shape[2]
    lowrank = adapter_up.shape[2]
    table_hits = (adapter_id[:, 0][:, None] == jnp.arange(owners, dtype=jnp.int32)[None, :]).astype(
        jnp.int32
    )
    home = jnp.sum(table_hits * owner_of[None, :], axis=1)
    member = (home[:, None] == jnp.arange(owners, dtype=jnp.int32)[None, :]).astype(jnp.int32)
    before = jnp.cumsum(member, axis=0) - member
    bucket_slot = jnp.sum(before * member, axis=1)
    mine = (home == own_index).astype(jnp.int32)
    matched = (bucket_slot[None, :] == jnp.arange(CAP, dtype=jnp.int32)[:, None]).astype(
        jnp.int32
    ) * mine[None, :]
    bucket_row = jnp.sum(matched * jnp.arange(row_count, dtype=jnp.int32)[None, :], axis=1)
    filled = jnp.sum(matched, axis=1)
    piece = lax.all_gather(tokens, "owner", axis=0, tiled=True)
    gate_out = jnp.dot(piece, base_weight[0], preferred_element_type=jnp.float32)
    up_out = jnp.dot(piece, base_weight[1], preferred_element_type=jnp.float32)
    fetched = jnp.take(piece, jnp.clip(bucket_row, 0, row_count - 1), axis=0)
    picked = jnp.where((filled > 0)[:, None], fetched.astype(jnp.float32), 0.0)
    codes = lax.dot_general(picked, adapter_down[0], (((1,), (1,)), ((), ())), precision=HIGHEST)
    factor_local = adapter_up[0].reshape(2, lowrank, owners, ff_dev)
    full_terms = jnp.einsum(
        "cpk,pkof->cpof",
        codes.reshape(CAP, 2, lowrank),
        factor_local,
        precision=HIGHEST,
    )
    full_terms = full_terms.astype(jnp.bfloat16)
    received = lax.all_to_all(full_terms, "owner", split_axis=2, concat_axis=2, tiled=True)
    adapter_term = received[bucket_slot, :, home, :].astype(jnp.float32)
    hidden = jax.nn.silu(gate_out + adapter_term[:, 0, :]) * (up_out + adapter_term[:, 1, :])
    return hidden.astype(jnp.bfloat16)


def split_two(value):
    high = value.astype(jnp.bfloat16)
    low = (value - high.astype(jnp.float32)).astype(jnp.bfloat16)
    return high, low


def iota(shape, dim):
    return lax.broadcasted_iota(jnp.int32, shape, dim)


def kernel(
    depth_z,
    width_y,
    id_ref,
    owner_ref,
    tok_hbm,
    w_hbm,
    down_hbm,
    up_hbm,
    out_ref,
    gathered,
    weights,
    down,
    up_wide,
    up_send,
    up_all,
    packed,
    total,
    code_total,
    local_sem,
    weight_sem,
    token_sem,
    send_sem,
    recv_sem,
    factor_send,
    factor_recv,
    code_send,
    code_recv,
):
    n = depth_z * width_y * 2
    chunks = gathered.shape[0]
    rows_dev = gathered.shape[2]
    wide = gathered.shape[3]
    rows = n * rows_dev
    ff = weights.shape[2]
    rank = up_all.shape[2]
    me = lax.axis_index("owner")
    core = lax.rem(me, 2)
    y = lax.rem(me // 2, width_y)
    z = me // (2 * width_y)

    def index(zz, yy, cc):
        return (zz * width_y + yy) * 2 + cc

    def peer(j):
        return lax.rem(me + j, n)

    def token_copy(c):
        return pltpu.make_async_copy(
            tok_hbm.at[:, pl.ds(c * wide, wide)], gathered.at[c, me], token_sem.at[c]
        )

    for c in range(chunks):
        token_copy(c).start()
    up_copy = pltpu.make_async_copy(up_hbm.at[0], up_wide, local_sem.at[0])
    up_copy.start()

    def weight_copy(c):
        part = pl.ds(pl.multiple_of(c * wide, wide), wide)
        return pltpu.make_async_copy(w_hbm.at[:, part], weights.at[:, part], weight_sem.at[c])

    for c in range(chunks):
        weight_copy(c).start()
    down_copy = pltpu.make_async_copy(down_hbm.at[0], down, local_sem.at[1])
    down_copy.start()

    barrier = pltpu.get_barrier_semaphore()
    for j in range(1, n):
        pl.semaphore_signal(
            barrier, inc=1, device_id={"owner": peer(j)}, device_id_type=pl.DeviceIdType.MESH
        )
    pl.semaphore_wait(barrier, n - 1)

    def block_copy(kind, c, o, target):
        return pltpu.make_async_remote_copy(
            src_ref=gathered.at[c, o],
            dst_ref=gathered.at[c, o],
            send_sem=send_sem.at[kind, c, o],
            recv_sem=recv_sem.at[c, o],
            device_id={"owner": target},
            device_id_type=pl.DeviceIdType.MESH,
        )

    def upward(c, o):
        return block_copy(0, c, o, index(lax.rem(z + 1, depth_z), y, core))

    def downward(c, o):
        return block_copy(1, c, o, index(lax.rem(z + depth_z - 1, depth_z), y, core))

    def across(c, o):
        return block_copy(2, c, o, index(z, 1 - y, core))

    def sibling(c, o):
        return block_copy(3, c, o, index(z, y, 1 - core))

    def own_sends(c):
        token_copy(c).wait()

        @pl.when(z < depth_z - 1)
        def _():
            upward(c, me).start()

        @pl.when(z > 0)
        def _():
            downward(c, me).start()

        if width_y > 1:
            across(c, me).start()
        sibling(c, me).start()

    def factor_copy(j):
        return pltpu.make_async_remote_copy(
            src_ref=up_send.at[peer(j)],
            dst_ref=up_all.at[:, me],
            send_sem=factor_send.at[j],
            recv_sem=factor_recv.at[j],
            device_id={"owner": peer(j)},
            device_id_type=pl.DeviceIdType.MESH,
        )

    def code_copy(j):
        return pltpu.make_async_remote_copy(
            src_ref=packed.at[me],
            dst_ref=packed.at[me],
            send_sem=code_send.at[j],
            recv_sem=code_recv.at[j],
            device_id={"owner": peer(j)},
            device_id_type=pl.DeviceIdType.MESH,
        )

    own_sends(0)
    up_copy.wait()
    for o in range(n):
        up_send[o] = up_wide[:, :, o * ff : (o + 1) * ff].astype(jnp.bfloat16)
    up_all[:, pl.ds(me, 1)] = up_send[pl.ds(me, 1)].reshape(2, 1, rank, ff)

    def relay(c):
        for d in range(1, depth_z):

            @pl.when(z >= d)
            def _():
                o = index(z - d, y, core)
                upward(c, o).wait_recv()

                @pl.when(z < depth_z - 1)
                def _():
                    upward(c, o).start()

                if width_y > 1:
                    across(c, o).start()
                sibling(c, o).start()

            @pl.when(z + d < depth_z)
            def _():
                o = index(z + d, y, core)
                downward(c, o).wait_recv()

                @pl.when(z > 0)
                def _():
                    downward(c, o).start()

                if width_y > 1:
                    across(c, o).start()
                sibling(c, o).start()

        if width_y > 1:
            for d in range(depth_z):
                o = index(lax.rem(z + d, depth_z), 1 - y, core)
                across(c, o).wait_recv()
                sibling(c, o).start()
        for zz in range(depth_z):
            for yy in range(width_y):
                sibling(c, index(zz, yy, 1 - core)).wait_recv()

    total[...] = jnp.zeros_like(total)
    code_total[...] = jnp.zeros_like(code_total)
    down_copy.wait()

    def multiply(c):
        part = pl.ds(pl.multiple_of(c * wide, wide), wide)
        weight_copy(c).wait()
        high, low = split_two(down[:, part])
        factors = jnp.concatenate([high] * 4 + [low] * 4, axis=0)
        code_total[...] += lax.dot_general(
            gathered[c].reshape(rows, wide),
            factors,
            (((1,), (1,)), ((), ())),
            preferred_element_type=jnp.float32,
        )
        for p in range(2):

            @pl.loop(0, ff // COLUMN_TILE)
            def _(t):
                columns = pl.ds(pl.multiple_of(t * COLUMN_TILE, COLUMN_TILE), COLUMN_TILE)
                total[p, :, columns] += jnp.dot(
                    gathered[c].reshape(rows, wide),
                    weights[p, part, columns],
                    preferred_element_type=jnp.float32,
                )

    per_step = -(-(n - 1) // chunks)
    for c in range(chunks):
        if c + 1 < chunks:
            own_sends(c + 1)
        for j in range(1 + c * per_step, min(n, 1 + (c + 1) * per_step)):
            factor_copy(j).start()
        relay(c)
        multiply(c)

    ids = id_ref[...]
    hit = ids == iota((rows, n), 1)
    home = jnp.sum(jnp.where(hit, owner_ref[...], 0).astype(jnp.float32), axis=1, keepdims=True)
    home = home.astype(jnp.int32)
    member = (home == iota((rows, 128), 1)).astype(jnp.float32)
    lower = (iota((rows, rows), 1) < iota((rows, rows), 0)).astype(jnp.bfloat16)
    before = jnp.dot(lower, member.astype(jnp.bfloat16), preferred_element_type=jnp.float32)
    slot = jnp.sum(before * member, axis=1, keepdims=True).astype(jnp.int32)
    slot_low, slot_high = lax.rem(slot, 8), slot // 8
    lane_group = iota((rows, 128), 1) // (2 * rank)
    codes = code_total[:, :128] + code_total[:, 128:]
    placed = jnp.where((lane_group == slot_high) & (home == me), codes, 0.0)
    pick = (slot_low == iota((rows, 8), 1)).astype(jnp.float32)
    packed[me] = lax.dot_general(
        pick, placed, (((0,), (0,)), ((), ())), precision=HIGHEST, preferred_element_type=jnp.float32
    )
    for j in range(1, n):
        code_copy(j).start()
    back = (home * 8 + slot_low == iota((rows, n * 8), 1)).astype(jnp.float32)
    for j in range(1, n):
        code_copy(j).wait()
    rows_codes = jnp.dot(
        back, packed[...].reshape(n * 8, 128), precision=HIGHEST, preferred_element_type=jnp.float32
    )
    rows_codes = jnp.where(lane_group == slot_high, rows_codes, 0.0)
    spread = []
    for p in range(2):
        place = lax.rem(iota((128, n * rank), 0), 2 * rank)
        place = place == p * rank + lax.rem(iota((128, n * rank), 1), rank)
        value = jnp.dot(
            rows_codes, place.astype(jnp.float32), precision=HIGHEST, preferred_element_type=jnp.float32
        )
        spread.append(split_two(jnp.where(iota((rows, n * rank), 1) // rank == home, value, 0.0)))

    for j in range(1, n):
        factor_copy(j).wait()

    def preact(p, lo, hi):
        factors = up_all[p].reshape(n * rank, ff)[:, lo:hi]
        term = jnp.dot(spread[p][0], factors, preferred_element_type=jnp.float32)
        term += jnp.dot(spread[p][1], factors, preferred_element_type=jnp.float32)
        return total[p, :, lo:hi] + term.astype(jnp.bfloat16).astype(jnp.float32)

    for lo in range(0, ff, COLUMN_TILE):
        gate = preact(0, lo, lo + COLUMN_TILE)
        up = preact(1, lo, lo + COLUMN_TILE)
        out_ref[:, lo : lo + COLUMN_TILE] = (gate / (1.0 + jnp.exp(-gate)) * up).astype(out_ref.dtype)

    for c in range(chunks):
        for zz in range(depth_z):
            o = index(zz, y, core)

            @pl.when((z < depth_z - 1) & (zz <= z))
            def _():
                upward(c, o).wait_send()

            @pl.when((z > 0) & (zz >= z))
            def _():
                downward(c, o).wait_send()

            if width_y > 1:
                across(c, o).wait_send()
            for yy in range(width_y):
                sibling(c, index(zz, yy, core)).wait_send()


def fused(depth_z, width_y, tokens, base_weight, adapter_down, adapter_up, adapter_id, owner_of):
    n = depth_z * width_y * 2
    rows_dev, d = tokens.shape
    ff = base_weight.shape[2]
    rank = adapter_up.shape[2]
    rows = rows_dev * n
    wide = d // CHUNKS
    any_space = pl.BlockSpec(memory_space=pl.ANY)
    vmem = pl.BlockSpec(memory_space=pltpu.VMEM)
    dma = pltpu.SemaphoreType.DMA
    return pl.pallas_call(
        functools.partial(kernel, depth_z, width_y),
        out_shape=jax.ShapeDtypeStruct((rows, ff), jnp.bfloat16),
        in_specs=[vmem, vmem, any_space, any_space, any_space, any_space],
        out_specs=vmem,
        scratch_shapes=[
            pltpu.VMEM((CHUNKS, n, rows_dev, wide), jnp.bfloat16),
            pltpu.VMEM((2, d, ff), jnp.bfloat16),
            pltpu.VMEM((2 * rank, d), jnp.float32),
            pltpu.VMEM((2, rank, n * ff), jnp.float32),
            pltpu.VMEM((n, 2, rank, ff), jnp.bfloat16),
            pltpu.VMEM((2, n, rank, ff), jnp.bfloat16),
            pltpu.VMEM((n, 8, 128), jnp.float32),
            pltpu.VMEM((2, rows, ff), jnp.float32),
            pltpu.VMEM((rows, 256), jnp.float32),
            dma((2,)),
            dma((CHUNKS,)),
            dma((CHUNKS,)),
            dma((4, CHUNKS, n)),
            dma((CHUNKS, n)),
            dma((n,)),
            dma((n,)),
            dma((n,)),
            dma((n,)),
        ],
        compiler_params=pltpu.CompilerParams(
            collective_id=0, has_side_effects=True, vmem_limit_bytes=60 * 1024 * 1024
        ),
        cost_estimate=pl.CostEstimate(
            flops=4 * rows * d * ff, bytes_accessed=4 * d * ff, transcendentals=rows * ff
        ),
    )(adapter_id, owner_of.reshape(1, n), tokens, base_weight, adapter_down, adapter_up)


def solution(mesh):
    owners = mesh.shape["owner"]
    width_y = 4 // mesh.shape["groups"]
    depth_z = owners // (2 * width_y)
    plan = functools.partial(fused, depth_z, width_y) if owners <= 16 else on_device
    return jax.shard_map(
        plan,
        mesh=mesh,
        in_specs=(
            P(("groups", "owner"), None),
            P(None, None, "owner"),
            P(("groups", "owner"), None, None),
            P(("groups", "owner"), None, None, None),
            P("groups", None),
            P("groups"),
        ),
        out_specs=P("groups", "owner"),
        check_vma=False,
    )
```

time: 162 us -> 107 us (0.66)
  the two profiles are of different devices: /device:TPU:13 before, /device:TPU:0 now
where the time goes in v1:
time: 107 us
  Pallas kernels  104 us (97%)
  local copies, waits for them, and re-layouts  3.34 us (3%)
    pallas_call x1, Pallas kernels, fused(): pl.pallas_call(functools.partial(kernel, depth_z, width_y), out_shape=jax...  104 us
    unnamed x2, local copies, waits for them, and re-layouts  3.34 us

profile of v1, /device:TPU:0, one launch (start us, length us, event | category | flops | bytes accessed | tf_op | source)
XLA Modules:
  0.0 107.0 jit_solution(7320284857919889494)
XLA Ops:
  0.0 1.5 %copy.7.id_ref = s32[256,1]{1,0:T(8,128)} copy(s32[256,1]{0,1:T(1,128)} %param.10) | data formatting | bytes 2048 | tf_op args[4]
  1.5 103.6 %shard_map.64 = bf16[256,1024]{1,0:T(8,128)(2,1)} custom-call(s32[256,1]{1,0:T(8,128)} %copy.7.id_ref, s32[1,16]{1,0:T(1,128)} %bitcast.1, bf16[16,8192]{1,0:T(8,128)(2,1)} %tok_hbm.1, bf16[2,8192,1024]{2,1,0:T(8,128)(2,1)} %w_hbm.1, f32[1,32,8192]{2,1,0:T(8,128)} %down_hbm.1, f32[1,2,16,16384]{3,2,1,0:T(8,128)} %up_hbm.1), custom_call_target="tpu_custom_call" | custom-call | flops 8589934592 | bytes 33554432 | tf_op jit(solution)/shard_map/pallas_call | solution.py:351
  105.1 1.9 %copy.9 = bf16[256,1024]{1,0:T(8,128)(2,1)} copy(bf16[256,1024]{1,0:T(8,128)(2,1)} %shard_map.64) | data formatting | bytes 1048576

commit v2 on v1

--- a/solution.py
+++ b/solution.py
@@ -9,7 +9,9 @@
 
 CAP = 32
 CHUNKS = 4
-COLUMN_TILE = 256
+COLUMN_TILE = 512
+FACTORS_PER_TICK = 15
+FACTOR_TICK = 4
 HIGHEST = lax.Precision.HIGHEST
 
 
@@ -193,46 +195,43 @@
             device_id_type=pl.DeviceIdType.MESH,
         )
 
-    own_sends(0)
+    for c in range(chunks):
+        own_sends(c)
     up_copy.wait()
     for o in range(n):
         up_send[o] = up_wide[:, :, o * ff : (o + 1) * ff].astype(jnp.bfloat16)
     up_all[:, pl.ds(me, 1)] = up_send[pl.ds(me, 1)].reshape(2, 1, rank, ff)
 
-    def relay(c):
-        for d in range(1, depth_z):
-
-            @pl.when(z >= d)
+    def hop(c, d):
+        for side, arrive, last in ((-1, upward, depth_z - 1), (1, downward, 0)):
+
+            @pl.when((z >= d) if side < 0 else (z + d < depth_z))
             def _():
-                o = index(z - d, y, core)
-                upward(c, o).wait_recv()
-
-                @pl.when(z < depth_z - 1)
+                o = index(z + side * d, y, core)
+                arrive(c, o).wait_recv()
+
+                @pl.when(z != last)
                 def _():
-                    upward(c, o).start()
+                    arrive(c, o).start()
 
                 if width_y > 1:
                     across(c, o).start()
                 sibling(c, o).start()
 
-            @pl.when(z + d < depth_z)
+    def land(c, d):
+        for zz, there in ((z - d, z >= d), (z + d, z + d < depth_z)):
+            there = there if d > 0 else z >= 0
+
+            @pl.when(there)
             def _():
-                o = index(z + d, y, core)
-                downward(c, o).wait_recv()
-
-                @pl.when(z > 0)
-                def _():
-                    downward(c, o).start()
-
-                if width_y > 1:
-                    across(c, o).start()
-                sibling(c, o).start()
-
-        if width_y > 1:
-            for d in range(depth_z):
-                o = index(lax.rem(z + d, depth_z), 1 - y, core)
+                o = index(zz, 1 - y, core)
                 across(c, o).wait_recv()
                 sibling(c, o).start()
+
+            if d == 0:
+                break
+
+    def complete(c):
         for zz in range(depth_z):
             for yy in range(width_y):
                 sibling(c, index(zz, yy, 1 - core)).wait_recv()
@@ -241,9 +240,8 @@
     code_total[...] = jnp.zeros_like(code_total)
     down_copy.wait()
 
-    def multiply(c):
+    def code_dot(c):
         part = pl.ds(pl.multiple_of(c * wide, wide), wide)
-        weight_copy(c).wait()
         high, low = split_two(down[:, part])
         factors = jnp.concatenate([high] * 4 + [low] * 4, axis=0)
         code_total[...] += lax.dot_general(
@@ -252,6 +250,10 @@
             (((1,), (1,)), ((), ())),
             preferred_element_type=jnp.float32,
         )
+
+    def multiply(c):
+        part = pl.ds(pl.multiple_of(c * wide, wide), wide)
+        weight_copy(c).wait()
         for p in range(2):
 
             @pl.loop(0, ff // COLUMN_TILE)
@@ -262,15 +264,6 @@
                     weights[p, part, columns],
                     preferred_element_type=jnp.float32,
                 )
-
-    per_step = -(-(n - 1) // chunks)
-    for c in range(chunks):
-        if c + 1 < chunks:
-            own_sends(c + 1)
-        for j in range(1 + c * per_step, min(n, 1 + (c + 1) * per_step)):
-            factor_copy(j).start()
-        relay(c)
-        multiply(c)
 
     ids = id_ref[...]
     hit = ids == iota((rows, n), 1)
@@ -282,15 +275,40 @@
     slot = jnp.sum(before * member, axis=1, keepdims=True).astype(jnp.int32)
     slot_low, slot_high = lax.rem(slot, 8), slot // 8
     lane_group = iota((rows, 128), 1) // (2 * rank)
-    codes = code_total[:, :128] + code_total[:, 128:]
-    placed = jnp.where((lane_group == slot_high) & (home == me), codes, 0.0)
     pick = (slot_low == iota((rows, 8), 1)).astype(jnp.float32)
-    packed[me] = lax.dot_general(
-        pick, placed, (((0,), (0,)), ((), ())), precision=HIGHEST, preferred_element_type=jnp.float32
-    )
-    for j in range(1, n):
-        code_copy(j).start()
     back = (home * 8 + slot_low == iota((rows, n * 8), 1)).astype(jnp.float32)
+
+    def share_codes():
+        codes = code_total[:, :128] + code_total[:, 128:]
+        placed = jnp.where((lane_group == slot_high) & (home == me), codes, 0.0)
+        packed[me] = lax.dot_general(
+            pick, placed, (((0,), (0,)), ((), ())), precision=HIGHEST, preferred_element_type=jnp.float32
+        )
+        for j in range(1, n):
+            code_copy(j).start()
+
+    def factors_of(tick):
+        first = 1 + max(0, tick - FACTOR_TICK) * FACTORS_PER_TICK
+        count = FACTORS_PER_TICK if tick >= FACTOR_TICK else 0
+        return range(first, n if tick == chunks + depth_z - 1 else min(n, first + count))
+
+    for tick in range(chunks + depth_z):
+        for d in range(1, depth_z):
+            if 0 <= tick - d + 1 < chunks:
+                hop(tick - d + 1, d)
+        if width_y > 1:
+            for d in range(depth_z):
+                if 0 <= tick - d < chunks:
+                    land(tick - d, d)
+        for j in factors_of(tick):
+            factor_copy(j).start()
+        if tick >= depth_z:
+            complete(tick - depth_z)
+            code_dot(tick - depth_z)
+            if tick == chunks + depth_z - 1:
+                share_codes()
+            multiply(tick - depth_z)
+
     for j in range(1, n):
         code_copy(j).wait()
     rows_codes = jnp.dot(

time: 107 us -> 65.5 us (0.61)
  Pallas kernels: 104 us -> 61.9 us
    pallas_call x1, Pallas kernels: 104 us -> 61.9 us  [fused(): pl.pallas_call(functools.partial(kernel, depth_z, width_y), out_shape=jax...]
where the time goes in v2:
time: 65.5 us; the launch traced here: 65.3 us
  Pallas kernels  61.9 us (95%)
  local copies, waits for them, and re-layouts  3.34 us (5%)
    pallas_call x1, Pallas kernels, fused(): pl.pallas_call(functools.partial(kernel, depth_z, width_y), out_shape=jax...  61.9 us
    unnamed x2, local copies, waits for them, and re-layouts  3.34 us

profile of v2, /device:TPU:0, one launch (start us, length us, event | category | flops | bytes accessed | tf_op | source)
XLA Modules:
  0.0 65.3 jit_solution(9979313285984131993)
XLA Ops:
  0.0 1.5 %copy.7.id_ref = s32[256,1]{1,0:T(8,128)} copy(s32[256,1]{0,1:T(1,128)} %param.10) | data formatting | bytes 2048 | tf_op args[4]
  1.5 61.9 %shard_map.64 = bf16[256,1024]{1,0:T(8,128)(2,1)} custom-call(s32[256,1]{1,0:T(8,128)} %copy.7.id_ref, s32[1,16]{1,0:T(1,128)} %bitcast.1, bf16[16,8192]{1,0:T(8,128)(2,1)} %tok_hbm.1, bf16[2,8192,1024]{2,1,0:T(8,128)(2,1)} %w_hbm.1, f32[1,32,8192]{2,1,0:T(8,128)} %down_hbm.1, f32[1,2,16,16384]{3,2,1,0:T(8,128)} %up_hbm.1), custom_call_target="tpu_custom_call" | custom-call | flops 8589934592 | bytes 33554432 | tf_op jit(solution)/shard_map/pallas_call | solution.py:369
  63.4 1.9 %copy.9 = bf16[256,1024]{1,0:T(8,128)(2,1)} copy(bf16[256,1024]{1,0:T(8,128)(2,1)} %shard_map.64) | data formatting | bytes 1048576

commit v3 on v2

--- a/solution.py
+++ b/solution.py
@@ -8,10 +8,10 @@
 from jax.sharding import PartitionSpec as P
 
 CAP = 32
-CHUNKS = 4
+CHUNKS = 2
 COLUMN_TILE = 512
 FACTORS_PER_TICK = 15
-FACTOR_TICK = 4
+FACTOR_TICK = 2
 HIGHEST = lax.Precision.HIGHEST
 
 
@@ -236,20 +236,19 @@
             for yy in range(width_y):
                 sibling(c, index(zz, yy, 1 - core)).wait_recv()
 
-    total[...] = jnp.zeros_like(total)
-    code_total[...] = jnp.zeros_like(code_total)
     down_copy.wait()
 
     def code_dot(c):
         part = pl.ds(pl.multiple_of(c * wide, wide), wide)
         high, low = split_two(down[:, part])
         factors = jnp.concatenate([high] * 4 + [low] * 4, axis=0)
-        code_total[...] += lax.dot_general(
+        value = lax.dot_general(
             gathered[c].reshape(rows, wide),
             factors,
             (((1,), (1,)), ((), ())),
             preferred_element_type=jnp.float32,
         )
+        code_total[...] = value if c == 0 else code_total[...] + value
 
     def multiply(c):
         part = pl.ds(pl.multiple_of(c * wide, wide), wide)
@@ -259,11 +258,12 @@
             @pl.loop(0, ff // COLUMN_TILE)
             def _(t):
                 columns = pl.ds(pl.multiple_of(t * COLUMN_TILE, COLUMN_TILE), COLUMN_TILE)
-                total[p, :, columns] += jnp.dot(
+                value = jnp.dot(
                     gathered[c].reshape(rows, wide),
                     weights[p, part, columns],
                     preferred_element_type=jnp.float32,
                 )
+                total[p, :, columns] = value if c == 0 else total[p, :, columns] + value
 
     ids = id_ref[...]
     hit = ids == iota((rows, n), 1)

time: 65.5 us -> 65 us (level)
  no operation moved by 1% of the time
where the time goes in v3:
time: 65 us; the launch traced here: 64.8 us
  Pallas kernels  61.4 us (94%)
  local copies, waits for them, and re-layouts  3.34 us (5%)
    pallas_call x1, Pallas kernels, fused(): pl.pallas_call(functools.partial(kernel, depth_z, width_y), out_shape=jax...  61.4 us
    unnamed x2, local copies, waits for them, and re-layouts  3.34 us

profile of v3, /device:TPU:0, one launch (start us, length us, event | category | flops | bytes accessed | tf_op | source)
XLA Modules:
  0.0 64.8 jit_solution(8571016424014006451)
XLA Ops:
  0.0 1.5 %copy.7.id_ref = s32[256,1]{1,0:T(8,128)} copy(s32[256,1]{0,1:T(1,128)} %param.10) | data formatting | bytes 2048 | tf_op args[4]
  1.5 61.4 %shard_map.64 = bf16[256,1024]{1,0:T(8,128)(2,1)} custom-call(s32[256,1]{1,0:T(8,128)} %copy.7.id_ref, s32[1,16]{1,0:T(1,128)} %bitcast.1, bf16[16,8192]{1,0:T(8,128)(2,1)} %tok_hbm.1, bf16[2,8192,1024]{2,1,0:T(8,128)(2,1)} %w_hbm.1, f32[1,32,8192]{2,1,0:T(8,128)} %down_hbm.1, f32[1,2,16,16384]{3,2,1,0:T(8,128)} %up_hbm.1), custom_call_target="tpu_custom_call" | custom-call | flops 8589934592 | bytes 33554432 | tf_op jit(solution)/shard_map/pallas_call | solution.py:369
  62.9 1.9 %copy.9 = bf16[256,1024]{1,0:T(8,128)(2,1)} copy(bf16[256,1024]{1,0:T(8,128)(2,1)} %shard_map.64) | data formatting | bytes 1048576
